TPU v7x, 32 devices: a whole 2x2x4 slice. The times are simulated.
32 devices in a mesh: row: 2 (over y), col: 4 (over x, core), layer: 4 (over z).
Axes of the slice: x: 2, y: 2, z: 4, core: 2. Of those that a mesh axis runs over, the one named last changes fastest.
Arguments:
- sign_iterate: bfloat16 [2048, 2048], P('row', 'col'), may hold values from -0.21875 to 0.21875
- square: bfloat16 [2048, 2048], P('row', 'col'), may hold values from -6 to 6
- pattern: int32 [16, 16], replicated, may hold values 0 or 1
- keep: int32 [16, 16], replicated, may hold values from 0 to 1, as said below
Outputs:
- product: bfloat16 [2048, 2048], P(('row', 'layer'), 'col')
Inputs may be any that keep to these rules, and one draw needn't show every extreme that they name: In every region of 2 block rows by 4 block columns, aligned to the output's shards along row+layer and col, exactly 6 blocks have keep 1.
All inputs are finite; a program needn't handle non-finite values.
Results may differ from a plain program's by a relative error of at most 0.001.
Values may be sent and summed in bfloat16 or wider, within the bound.
A program may use at most 64 MiB of HBM per device.

v0:
```python
import jax
import jax.numpy as jnp
from jax import lax
from jax.sharding import PartitionSpec as P

BLK = 128


def apply_blocks(matrix, mask):
    nrow = mask.shape[0]
    ncol = mask.shape[1]
    shaped = matrix.reshape(nrow, BLK, ncol, BLK)
    chosen = (mask == 1)[:, None, :, None]
    return jnp.where(chosen, shaped, jnp.zeros_like(shaped)).reshape(matrix.shape)


def shards(sign_iterate, square, pattern, keep):
    layers = lax.axis_size("layer")
    layer_idx = lax.axis_index("layer")
    row_idx = lax.axis_index("row")
    col_idx = lax.axis_index("col")
    rows, cols = sign_iterate.shape
    span = cols // layers
    own_cols = lax.dynamic_slice_in_dim(sign_iterate, layer_idx * span, span, 1)
    first_col = (col_idx * layers + layer_idx) * (span // BLK)
    own_mask = lax.dynamic_slice(
        pattern, (row_idx * (rows // BLK), first_col), (rows // BLK, span // BLK)
    )
    stored = apply_blocks(own_cols, own_mask)
    sq_rows, sq_cols = square.shape
    groups = sq_rows // (span * layers)
    shaped = square.reshape(groups, layers, span, sq_cols)
    own_rows = lax.dynamic_index_in_dim(shaped, layer_idx, 1, False).reshape(groups * span, sq_cols)
    square_all = lax.all_gather(own_rows, "row", axis=0, tiled=True)
    partial_value = jnp.dot(
        lax.all_gather(stored, "col", axis=1, tiled=True),
        square_all,
        preferred_element_type=jnp.float32,
    )
    out_rows = rows // layers
    region_rows = out_rows // BLK
    region_cols = sq_cols // BLK
    first_row = (row_idx * layers + layer_idx) * region_rows
    keep_here = lax.dynamic_slice(
        keep, (first_row, col_idx * region_cols), (region_rows, region_cols)
    )
    count = region_rows * region_cols
    kept_count = 3 * count // 4
    keep_all = lax.dynamic_slice(
        keep,
        (row_idx * layers * region_rows, col_idx * region_cols),
        (layers * region_rows, region_cols),
    )
    flags = keep_all.reshape(layers, count)
    order = jnp.argsort(1 - flags, axis=1, stable=True)[:, :kept_count]
    blocks = (
        partial_value.reshape(layers, region_rows, BLK, region_cols, BLK)
        .transpose(0, 1, 3, 2, 4)
        .reshape(layers, count, BLK, BLK)
    )
    packed = jnp.take_along_axis(blocks, order[:, :, None, None], axis=1)
    reduced = lax.psum_scatter(packed, "layer", scatter_dimension=0, tiled=True)
    mine = lax.dynamic_index_in_dim(order, layer_idx, 0, False)
    unpacked = jnp.zeros((count, BLK, BLK), jnp.float32).at[mine].set(reduced[0])
    summed = (
        unpacked.reshape(region_rows, region_cols, BLK, BLK)
        .transpose(0, 2, 1, 3)
        .reshape(out_rows, sq_cols)
    )
    return apply_blocks(summed, keep_here).astype(jnp.bfloat16)


def solution(mesh):
    return jax.shard_map(
        shards,
        mesh=mesh,
        in_specs=(P("row", "col"), P("row", "col"), P(), P()),
        out_specs=P(("row", "layer"), "col"),
        check_vma=False,
    )
```

profile of v0, /device:TPU:0, one launch (start us, length us, event | category | flops | bytes accessed | tf_op | source)
XLA Modules:
  0.0 84.7 jit_solution(3659014565282380108)
XLA Ops:
  6.5 0.0 copy-start
  6.5 0.0 all-gather.2.cloned.1.call-start
  6.5 1.0 %fusion.1 = pred[8]{0:T(512)(128)(4,1)S(1)} fusion(s32[16,16]{1,0:T(8,128)} %param.6, s32[]{:T(128)S(6)} %select_n.56, s32[]{:T(128)S(6)} %select_n.60), kind=kLoop, calls=%fused_computation.12 | loop fusion | flops 8 | bytes 48 | tf_op jit(solution)/shard_map/eq | solution.py:13
  7.5 0.1 broadcast_bitcast_fusion
  7.6 1.9 %dynamic-slice_select_fusion = bf16[1024,128]{1,0:T(8,128)(2,1)} fusion(bf16[1024,512]{1,0:T(8,128)(2,1)} %param.4, s32[]{:T(128)S(6)} %select_n.61, pred[1024]{0:T(1024)(128)(4,1)S(1)} %broadcast_bitcast_fusion), kind=kLoop, calls=%fused_computation.6 | loop fusion | flops 131072 | bytes 525316 | tf_op jit(solution)/shard_map/jit(_where)/select_n | solution.py:14
  9.4 0.0 all-gather.2.cloned.1.call-update
  9.5 0.0 reduce-scatter.2.cloned.1.call-start
  9.5 0.8 dynamic-slice_subtract_fusion
  10.3 0.1 sub.11
  10.4 0.1 copy.9
  10.4 0.6 sort.17
  11.1 0.1 copy.10
  11.2 0.1 copy.12
  11.3 0.1 reshape.85
  11.4 0.0 copy-done
  11.4 10.0 %all_gather.7 = bf16[512,512]{1,0:T(8,128)(2,1)} all-gather(bf16[256,512]{1,0:T(8,128)(2,1)S(1)} %bitcast.32), channel_id=1, replica_groups=mesh['row'=2,'col'=4,'layer'=4] {'row'}, dimensions={0}, use_global_device_ids=true | all-gather | bytes 786432 | tf_op jit(solution)/shard_map/all_gather | solution.py:34
  21.5 7.7 %all-gather.2.cloned.1.call-done = bf16[1024,512]{1,0:T(8,128)(2,1)} async-done(((bf16[1024,128]{1,0:T(8,128)(2,1)}), bf16[1024,512]{1,0:T(8,128)(2,1)}) %all-gather.2.cloned.1.call-update) | async-done | bytes 1048592 | tf_op jit(solution)/shard_map/all_gather | solution.py:36
  29.2 2.1 %fusion.3 = f32[1024,512]{1,0:T(8,128)S(1)} fusion(bf16[1024,512]{1,0:T(8,128)(2,1)} %all-gather.2.cloned.1.call-done, bf16[512,512]{1,0:T(8,128)(2,1)} %all_gather.7), kind=kOutput, calls=%fused_computation.20 | convolution fusion | flops 536870912 | bytes 3670016 | tf_op jit(solution)/shard_map/dot_general | solution.py:35
  31.3 1.8 %reshape.81 = f32[4,2,128,4,128]{4,3,2,1,0:T(4,128)} reshape(f32[1024,512]{1,0:T(8,128)S(1)} %fusion.3) | data formatting | bytes 4194304 | tf_op jit(solution)/shard_map/reshape | solution.py:57
  33.1 1.9 %copy.11 = f32[4,2,128,4,128]{4,2,3,1,0:T(8,128)S(1)} copy(f32[4,2,128,4,128]{4,3,2,1,0:T(4,128)} %reshape.81) | data formatting | bytes 4194304 | tf_op jit(solution)/shard_map/reshape | solution.py:57
  34.9 1.9 %gather_fusion = f32[24,128,128]{2,1,0:T(8,128)} fusion(f32[4,8,128,128]{3,2,1,0:T(8,128)S(1)} %bitcast.29, s32[24]{0:T(128)S(1)} %reshape.85), kind=kCustom, calls=%fused_computation | custom fusion | bytes 3145920 | tf_op jit(solution)/shard_map/jit(take_along_axis)/gather | solution.py:61
  36.9 2.7 %broadcast_select_fusion = f32[4,6,128,128]{3,2,1,0:T(8,128)} fusion(f32[4,6,128,128]{3,2,1,0:T(8,128)} %bitcast.30, pred[4,6]{1,0:T(4,128)(4,1)S(1)} %copy.10), kind=kLoop, calls=%fused_computation.2 | loop fusion | flops 393216 | bytes 3145752 | tf_op jit(solution)/shard_map/jit(take_along_axis)/select_n | solution.py:61
  39.6 0.0 reduce-scatter.2.cloned.1.call-update
  39.6 0.2 dynamic-slice_reduce_fusion
  39.8 0.8 dynamic-slice_compare_fusion.1
  40.6 34.5 %reduce-scatter.2.cloned.1.call-done = f32[1,6,128,128]{3,2,1,0:T(8,128)} async-done(((f32[4,6,128,128]{3,2,1,0:T(8,128)}), f32[1,6,128,128]{3,2,1,0:T(8,128)}) %reduce-scatter.2.cloned.1.call-update) | async-done | bytes 393232 | tf_op jit(solution)/shard_map/reduce_scatter | solution.py:62
  75.1 1.7 %scatter_fusion = f32[8,128,128]{2,1,0:T(8,128)S(1)} fusion(f32[8,128,128]{2,1,0:T(8,128)S(1)} %broadcast_in_dim.44, s32[6]{0:T(128)S(1)} %fusion.2, f32[6,128,128]{2,1,0:T(8,128)} %bitcast.34), kind=kCustom, calls=%fused_computation.1 | custom fusion | bytes 1179672 | tf_op jit(solution)/shard_map/scatter | solution.py:64
  76.8 0.1 fusion
  76.9 0.2 copy.13
  77.1 0.7 copy.16
  (7 shorter events, 0.1 us)
Async XLA Ops:
  6.5 4.9 %copy-start = (bf16[1024,512]{1,0:T(8,128)(2,1)S(1)}, bf16[1024,512]{1,0:T(8,128)(2,1)}, u32[]{:S(2)}) copy-start(bf16[1024,512]{1,0:T(8,128)(2,1)} %param.5) | copy-start | bytes 3145732
  6.5 22.7 %all-gather.2.cloned.1.call-start = ((), (), s32[]{:S(2)}) async-start(), calls=%async_computation.1 | async-start | bytes 1310720 | tf_op jit(solution)/shard_map/all_gather | solution.py:36
  9.5 65.6 %reduce-scatter.2.cloned.1.call-start = ((), (), s32[]{:S(2)}) async-start(), calls=%async_computation.2 | async-start | bytes 1966080 | tf_op jit(solution)/shard_map/reduce_scatter | solution.py:62
Sparse Core Ops, SparseCore 0:
  9.6 19.5 all-gather.1
  39.7 35.2 reduce-scatter.1
where the time goes:
time: 85.1 us; the launch traced here: 84.7 us
  waiting for transfers between devices  42.3 us (50%)
  between operations  13.5 us (16%)
  blocking collectives  10 us (12%)
  local copies, waits for them, and re-layouts  9.01 us (11%)
  other arithmetic  7.87 us (9%)
  matrix products  2.05 us (2%)
    reduce_scatter x1, waiting for transfers between devices, shards(): reduced = lax.psum_scatter(packed, 'layer', scatter_dimension=0, tiled=True)  34.5 us
    all_gather x1, blocking collectives, shards(): square_all = lax.all_gather(own_rows, 'row', axis=0, tiled=True)  10 us
    all_gather x1, waiting for transfers between devices, shards(): lax.all_gather(stored, 'col', axis=1, tiled=True)  7.74 us
    reshape x2, local copies, waits for them, and re-layouts, shards(): partial_value.reshape(layers, region_rows, BLK, region_cols, BLK)  3.65 us
    select_n x1, other arithmetic, shards(): packed = jnp.take_along_axis(blocks, order[:, :, None, None], axis=1)  2.73 us
    gather x3, local copies, waits for them, and re-layouts, shards(): packed = jnp.take_along_axis(blocks, order[:, :, None, None], axis=1)  2.12 us
    dot_general x1, matrix products, shards(): jnp.dot(lax.all_gather(stored, 'col', axis=1, tiled=True), square_all, pr...  2.05 us
    select_n x1, other arithmetic, apply_blocks(): jnp.where(chosen, shaped, jnp.zeros_like(shaped)).reshape(matrix.shape)  1.86 us
  transfers between devices with their start and end apart: 2, of which 2 were waited for; matrix products, arithmetic and copies ran while one was open for 3% of the time, Pallas kernels for 0%

commit v1 on v0

v1 whole, which is shorter than its diff:
```python
import functools

import jax
import jax.numpy as jnp
from jax import lax
from jax.experimental import pallas as pl
from jax.experimental.pallas import tpu as pltpu
from jax.sharding import PartitionSpec as P

BLK = 128
GROUP = 256
PIECES = 4
MESH = pl.DeviceIdType.MESH


def kernel(
    n_row,
    n_col,
    n_layer,
    x_ref,
    s_ref,
    pattern_ref,
    keep_ref,
    o_ref,
    xbuf,
    xm,
    sbuf,
    acc,
    local_sem,
    y_send,
    y_recv,
    z_send,
    z_recv,
    x_send,
    x_recv,
    c_send,
    c_recv,
):
    row = lax.axis_index("row")
    col = lax.axis_index("col")
    layer = lax.axis_index("layer")
    _, m, kc = xbuf.shape
    _, sr, n = sbuf.shape
    n_group = sr // GROUP
    ch = GROUP // PIECES
    n_chunk = n_group * PIECES
    half = lax.rem(layer, 2)
    mate_layer = layer + 1 - 2 * half
    core = lax.rem(col, 2)
    mate_col = col + 1 - 2 * core
    n_chip = n_col // 2
    relayed = n_chunk // 2 - 1
    direct = n_chunk - relayed

    def peer_row(d):
        return lax.rem(row + d, n_row)

    def from_row(d):
        return lax.rem(row + n_row - d, n_row)

    def peer_col(e):
        return lax.rem(col + 2 * e, n_col)

    def from_col(e):
        return lax.rem(col + n_col - 2 * e, n_col)

    x_own = x_ref.at[pl.ds(pl.multiple_of(layer * m, m), m), :]
    copy_x = pltpu.make_async_copy(x_own, xbuf.at[col], local_sem.at[0])
    copy_s = pltpu.make_async_copy(s_ref, sbuf.at[row], local_sem.at[1])

    barrier = pltpu.get_barrier_semaphore()
    peers = [{"row": peer_row(d)} for d in range(1, n_row)]
    peers += [{"col": peer_col(e)} for e in range(1, n_chip)]
    peers += [{"layer": mate_layer}, {"col": mate_col}]
    for peer in peers:
        pl.semaphore_signal(barrier, inc=1, device_id=peer, device_id_type=MESH)
    copy_x.start()
    copy_s.start()
    pl.semaphore_wait(barrier, len(peers))

    def chunk_at(j, h):
        return pl.ds(pl.multiple_of((j + h * (n_chunk - 1 - 2 * j)) * ch, ch), ch)

    y = {}
    for j in range(direct):
        for d in range(1, n_row):
            rows = chunk_at(j, half)
            y[d, j] = pltpu.make_async_remote_copy(
                src_ref=s_ref.at[rows, :],
                dst_ref=sbuf.at[row, rows, :],
                send_sem=y_send.at[d - 1, j],
                recv_sem=y_recv.at[d - 1, j],
                device_id={"row": peer_row(d)},
                device_id_type=MESH,
            )
            y[d, j].start()
        if j == 0:
            xs = {}
            for e in range(1, n_chip):
                xs[e] = pltpu.make_async_remote_copy(
                    src_ref=x_own,
                    dst_ref=xbuf.at[col],
                    send_sem=x_send.at[e - 1],
                    recv_sem=x_recv.at[e - 1],
                    device_id={"col": peer_col(e)},
                    device_id_type=MESH,
                )
                xs[e].start()
            cs = {}
            cs[0] = pltpu.make_async_remote_copy(
                src_ref=x_own,
                dst_ref=xbuf.at[col],
                send_sem=c_send.at[0],
                recv_sem=c_recv.at[0],
                device_id={"col": mate_col},
                device_id_type=MESH,
            )
            cs[0].start()

    z = {}

    def land(j):
        for d in range(1, n_row):
            y[d, j].wait_recv()
            if j < relayed:
                place = sbuf.at[from_row(d), chunk_at(j, half), :]
                z[d, j] = pltpu.make_async_remote_copy(
                    src_ref=place,
                    dst_ref=place,
                    send_sem=z_send.at[d - 1, j],
                    recv_sem=z_recv.at[d - 1, j],
                    device_id={"layer": mate_layer},
                    device_id_type=MESH,
                )
                z[d, j].start()

    def pass_x():
        for e in range(1, n_chip):
            xs[e].wait_recv()
            place = xbuf.at[from_col(e)]
            cs[e] = pltpu.make_async_remote_copy(
                src_ref=place,
                dst_ref=place,
                send_sem=c_send.at[e],
                recv_sem=c_recv.at[e],
                device_id={"col": mate_col},
                device_id_type=MESH,
            )
            cs[e].start()

    first_row = (row * n_layer + layer) * (m // BLK)

    def mask_x():
        copy_x.wait()
        for e in range(n_chip):
            cs[e].wait_recv()
        for c in range(n_col):
            for a in range(m // BLK):
                for b in range(kc // BLK):
                    stored = pattern_ref[first_row + a, c * (kc // BLK) + b]
                    flags = jnp.full((BLK, BLK), stored, jnp.int32) == 1
                    piece = xbuf[c, a * BLK : (a + 1) * BLK, b * BLK : (b + 1) * BLK]
                    g, at = divmod(c * kc + b * BLK, GROUP)
                    xm[g, a * BLK : (a + 1) * BLK, at : at + BLK] = jnp.where(
                        flags, piece.astype(jnp.float32), 0.0
                    ).astype(jnp.bfloat16)

    def term(owner, g):
        rows = pl.ds(pl.multiple_of(g * GROUP, GROUP), GROUP)
        return jnp.dot(
            xm[owner * n_group + g], sbuf[owner, rows, :], preferred_element_type=jnp.float32
        )

    def group_of(i, h):
        return i + h * (n_group - 1 - 2 * i)

    done = 0
    x_passed = masked = False
    for j in range(direct):
        land(j)
        if j == direct // 2 - 1:
            pass_x()
            x_passed = True
        if j == direct // 2 + 1:
            mask_x()
            copy_s.wait()
            acc[...] = sum((term(row, g) for g in range(1, n_group)), term(row, 0))
            masked = True
        if x_passed and masked and j < direct - 1:
            while (done + 1) * PIECES <= j + 1:
                for d in range(1, n_row):
                    acc[...] += term(from_row(d), group_of(done, half))
                done += 1
    for i in range(n_group // 2 - 1):
        for d in range(1, n_row):
            for j in range(i * PIECES, (i + 1) * PIECES):
                z[d, j].wait_recv()
            acc[...] += term(from_row(d), group_of(i, 1 - half))
    last = n_group // 2 - 1
    for d in range(1, n_row):
        for j in range(last * PIECES, relayed):
            z[d, j].wait_recv()
        total = acc[...] + term(from_row(d), group_of(last, 1 - half))
        if d < n_row - 1:
            acc[...] = total

    for a in range(m // BLK):
        for b in range(n // BLK):
            kept = keep_ref[first_row + a, col * (n // BLK) + b]
            flags = jnp.full((BLK, BLK), kept, jnp.int32) == 1
            piece = total[a * BLK : (a + 1) * BLK, b * BLK : (b + 1) * BLK]
            o_ref[a * BLK : (a + 1) * BLK, b * BLK : (b + 1) * BLK] = jnp.where(
                flags, piece, 0.0
            ).astype(o_ref.dtype)

    for group in (y, z, xs, cs):
        for copy in group.values():
            copy.wait_send()


def shards(sign_iterate, square, pattern, keep):
    n_row, n_col, n_layer = (lax.axis_size(a) for a in ("row", "col", "layer"))
    rows, kc = sign_iterate.shape
    sr, n = square.shape
    m = rows // n_layer
    n_chunk = sr // GROUP * PIECES
    relayed = n_chunk // 2 - 1
    direct = n_chunk - relayed
    dma = pltpu.SemaphoreType.DMA
    order = n_col * kc
    return pl.pallas_call(
        functools.partial(kernel, n_row, n_col, n_layer),
        out_shape=jax.ShapeDtypeStruct((m, n), jnp.bfloat16),
        in_specs=[
            pl.BlockSpec(memory_space=pl.ANY),
            pl.BlockSpec(memory_space=pl.ANY),
            pl.BlockSpec(memory_space=pltpu.SMEM),
            pl.BlockSpec(memory_space=pltpu.SMEM),
        ],
        out_specs=pl.BlockSpec(memory_space=pltpu.VMEM),
        scratch_shapes=[
            pltpu.VMEM((n_col, m, kc), jnp.bfloat16),
            pltpu.VMEM((order // GROUP, m, GROUP), jnp.bfloat16),
            pltpu.VMEM((n_row, sr, n), jnp.bfloat16),
            pltpu.VMEM((m, n), jnp.float32),
            dma((2,)),
            dma((n_row - 1, direct)),
            dma((n_row - 1, direct)),
            dma((n_row - 1, relayed)),
            dma((n_row - 1, relayed)),
            dma((n_col // 2 - 1,)),
            dma((n_col // 2 - 1,)),
            dma((n_col // 2,)),
            dma((n_col // 2,)),
        ],
        compiler_params=pltpu.CompilerParams(
            collective_id=0, has_side_effects=True, vmem_limit_bytes=56 * 2**20
        ),
        cost_estimate=pl.CostEstimate(
            flops=2 * m * n * order,
            bytes_accessed=2 * (m * kc + sr * n + m * n),
            transcendentals=0,
        ),
    )(sign_iterate, square, pattern, keep)


def solution(mesh):
    return jax.shard_map(
        shards,
        mesh=mesh,
        in_specs=(P("row", "col"), P("row", "col"), P(), P()),
        out_specs=P(("row", "layer"), "col"),
        check_vma=False,
    )
```

time: 85.1 us -> 24.1 us (0.28)
  waiting for transfers between devices: 42.3 us -> 0 us
  Pallas kernels: 0 us -> 22.1 us
  between operations: 13.5 us -> 0.01 us
  blocking collectives: 10 us -> 0 us
  other arithmetic: 7.87 us -> 0 us
  local copies, waits for them, and re-layouts: 9.01 us -> 1.67 us
  matrix products: 2.05 us -> 0 us
    reduce_scatter x1 -> x0, waiting for transfers between devices: 34.5 us -> none  [shards(): reduced = lax.psum_scatter(packed, 'layer', scatter_dimension=0, tiled=True)]
    pallas_call x0 -> x1, Pallas kernels: none -> 22.1 us  [shards(): pl.pallas_call(functools.partial(kernel, n_row, n_col, n_layer), out_shap...]
    all_gather x1 -> x0, blocking collectives: 10 us -> none  [shards(): square_all = lax.all_gather(own_rows, 'row', axis=0, tiled=True)]
    all_gather x1 -> x0, waiting for transfers between devices: 7.74 us -> none  [shards(): lax.all_gather(stored, 'col', axis=1, tiled=True)]
    select_n x3 -> x0, other arithmetic: 4.59 us -> none  [the longest x1 2.73 us: shards(): packed = jnp.take_along_axis(blocks, order[:, :, None, None], axis=1)]
    reshape x2 -> x0, local copies, waits for them, and re-layouts: 3.65 us -> none  [shards(): partial_value.reshape(layers, region_rows, BLK, region_cols, BLK)]
    gather x3 -> x0, local copies, waits for them, and re-layouts: 2.12 us -> none  [shards(): packed = jnp.take_along_axis(blocks, order[:, :, None, None], axis=1)]
    dot_general x1 -> x0, matrix products: 2.05 us -> none  [shards(): jnp.dot(lax.all_gather(stored, 'col', axis=1, tiled=True), square_all, pr...]
  transfers between devices with their start and end apart: 2 -> 0, of which waited for: 2 -> 0; matrix products, arithmetic and copies ran while one was open for 3% -> 0% of each run, Pallas kernels for 0% -> 0%
where the time goes in v1:
time: 24.1 us; the launch traced here: 23.8 us
  Pallas kernels  22.1 us (92%)
  local copies, waits for them, and re-layouts  1.67 us (7%)
    pallas_call x1, Pallas kernels, shards(): pl.pallas_call(functools.partial(kernel, n_row, n_col, n_layer), out_shap...  22.1 us
    unnamed x1, local copies, waits for them, and re-layouts  1.67 us

profile of v1, /device:TPU:0, one launch (start us, length us, event | category | flops | bytes accessed | tf_op | source)
XLA Modules:
  0.0 23.8 jit_solution(8521356537887013869)
XLA Ops:
  0.0 22.1 %shard_map.46 = bf16[256,512]{1,0:T(8,128)(2,1)} custom-call(bf16[1024,512]{1,0:T(8,128)(2,1)} %x_ref.1, bf16[1024,512]{1,0:T(8,128)(2,1)} %s_ref.1, s32[16,16]{1,0:T(8,128)} %pattern_ref.1, s32[16,16]{1,0:T(8,128)} %keep_ref.1), custom_call_target="tpu_custom_call" | custom-call | flops 536870912 | bytes 1572864 | tf_op jit(solution)/shard_map/pallas_call | solution.py:231
  22.1 1.7 %copy.6 = bf16[256,512]{1,0:T(8,128)(2,1)} copy(bf16[256,512]{1,0:T(8,128)(2,1)} %shard_map.46) | data formatting | bytes 524288

commit v2 on v1

--- a/solution.py
+++ b/solution.py
@@ -9,7 +9,7 @@
 
 BLK = 128
 GROUP = 256
-PIECES = 4
+PIECES = 2
 MESH = pl.DeviceIdType.MESH
 
 
@@ -19,9 +19,11 @@
     n_layer,
     x_ref,
     s_ref,
+    pattern_hbm,
+    keep_hbm,
+    o_ref,
     pattern_ref,
     keep_ref,
-    o_ref,
     xbuf,
     xm,
     sbuf,
@@ -76,6 +78,10 @@
         pl.semaphore_signal(barrier, inc=1, device_id=peer, device_id_type=MESH)
     copy_x.start()
     copy_s.start()
+    copy_pattern = pltpu.make_async_copy(pattern_hbm, pattern_ref, local_sem.at[2])
+    copy_keep = pltpu.make_async_copy(keep_hbm, keep_ref, local_sem.at[3])
+    copy_pattern.start()
+    copy_keep.start()
     pl.semaphore_wait(barrier, len(peers))
 
     def chunk_at(j, h):
@@ -152,6 +158,8 @@
 
     def mask_x():
         copy_x.wait()
+        copy_pattern.wait()
+        copy_keep.wait()
         for e in range(n_chip):
             cs[e].wait_recv()
         for c in range(n_col):
@@ -230,20 +238,22 @@
     order = n_col * kc
     return pl.pallas_call(
         functools.partial(kernel, n_row, n_col, n_layer),
-        out_shape=jax.ShapeDtypeStruct((m, n), jnp.bfloat16),
+        out_shape=pltpu.VMEM((m, n), jnp.bfloat16),
         in_specs=[
             pl.BlockSpec(memory_space=pl.ANY),
             pl.BlockSpec(memory_space=pl.ANY),
-            pl.BlockSpec(memory_space=pltpu.SMEM),
-            pl.BlockSpec(memory_space=pltpu.SMEM),
+            pl.BlockSpec(memory_space=pl.ANY),
+            pl.BlockSpec(memory_space=pl.ANY),
         ],
         out_specs=pl.BlockSpec(memory_space=pltpu.VMEM),
         scratch_shapes=[
+            pltpu.SMEM(pattern.shape, pattern.dtype),
+            pltpu.SMEM(keep.shape, keep.dtype),
             pltpu.VMEM((n_col, m, kc), jnp.bfloat16),
             pltpu.VMEM((order // GROUP, m, GROUP), jnp.bfloat16),
             pltpu.VMEM((n_row, sr, n), jnp.bfloat16),
             pltpu.VMEM((m, n), jnp.float32),
-            dma((2,)),
+            dma((4,)),
             dma((n_row - 1, direct)),
             dma((n_row - 1, direct)),
             dma((n_row - 1, relayed)),

time: 24.1 us -> 20.7 us (0.86)
  Pallas kernels: 22.1 us -> 19.8 us
  local copies, waits for them, and re-layouts: 1.67 us -> 0.71 us
    pallas_call x1, Pallas kernels: 22.1 us -> 19.8 us  [shards(): pl.pallas_call(functools.partial(kernel, n_row, n_col, n_layer), out_shap...]
    unnamed x1, local copies, waits for them, and re-layouts: 1.67 us -> 0.71 us
where the time goes in v2:
time: 20.7 us; the launch traced here: 20.5 us
  Pallas kernels  19.8 us (96%)
  local copies, waits for them, and re-layouts  0.71 us (3%)
    pallas_call x1, Pallas kernels, shards(): pl.pallas_call(functools.partial(kernel, n_row, n_col, n_layer), out_shap...  19.8 us
    unnamed x1, local copies, waits for them, and re-layouts  0.71 us

profile of v2, /device:TPU:0, one launch (start us, length us, event | category | flops | bytes accessed | tf_op | source)
XLA Modules:
  0.0 20.5 jit_solution(13770809473657075400)
XLA Ops:
  0.0 19.8 %shard_map.46 = bf16[256,512]{1,0:T(8,128)(2,1)S(1)} custom-call(bf16[1024,512]{1,0:T(8,128)(2,1)} %x_ref.1, bf16[1024,512]{1,0:T(8,128)(2,1)} %s_ref.1, s32[16,16]{1,0:T(8,128)} %pattern_hbm.1, s32[16,16]{1,0:T(8,128)} %keep_hbm.1), custom_call_target="tpu_custom_call" | custom-call | flops 536870912 | bytes 1572864 | tf_op jit(solution)/shard_map/pallas_call | solution.py:239
  19.8 0.7 %copy.6 = bf16[256,512]{1,0:T(8,128)(2,1)} copy(bf16[256,512]{1,0:T(8,128)(2,1)S(1)} %shard_map.46) | data formatting | bytes 524288

commit v3 on v2

--- a/solution.py
+++ b/solution.py
@@ -9,7 +9,7 @@
 
 BLK = 128
 GROUP = 256
-PIECES = 2
+PIECES = 8
 MESH = pl.DeviceIdType.MESH
 
 
@@ -51,7 +51,7 @@
     core = lax.rem(col, 2)
     mate_col = col + 1 - 2 * core
     n_chip = n_col // 2
-    relayed = n_chunk // 2 - 1
+    relayed = n_chunk // 2 - 3
     direct = n_chunk - relayed
 
     def peer_row(d):
@@ -83,6 +83,7 @@
     copy_pattern.start()
     copy_keep.start()
     pl.semaphore_wait(barrier, len(peers))
+    copy_s.wait()
 
     def chunk_at(j, h):
         return pl.ds(pl.multiple_of((j + h * (n_chunk - 1 - 2 * j)) * ch, ch), ch)
@@ -92,7 +93,7 @@
         for d in range(1, n_row):
             rows = chunk_at(j, half)
             y[d, j] = pltpu.make_async_remote_copy(
-                src_ref=s_ref.at[rows, :],
+                src_ref=sbuf.at[row, rows, :],
                 dst_ref=sbuf.at[row, rows, :],
                 send_sem=y_send.at[d - 1, j],
                 recv_sem=y_recv.at[d - 1, j],
@@ -186,12 +187,11 @@
     x_passed = masked = False
     for j in range(direct):
         land(j)
-        if j == direct // 2 - 1:
+        if j == relayed - 3:
             pass_x()
             x_passed = True
-        if j == direct // 2 + 1:
+        if j == relayed:
             mask_x()
-            copy_s.wait()
             acc[...] = sum((term(row, g) for g in range(1, n_group)), term(row, 0))
             masked = True
         if x_passed and masked and j < direct - 1:
@@ -232,7 +232,7 @@
     sr, n = square.shape
     m = rows // n_layer
     n_chunk = sr // GROUP * PIECES
-    relayed = n_chunk // 2 - 1
+    relayed = n_chunk // 2 - 3
     direct = n_chunk - relayed
     dma = pltpu.SemaphoreType.DMA
     order = n_col * kc

time: 20.7 us -> 20.4 us (0.986)
  Pallas kernels: 19.8 us -> 19.5 us
    pallas_call x1, Pallas kernels: 19.8 us -> 19.5 us  [shards(): pl.pallas_call(functools.partial(kernel, n_row, n_col, n_layer), out_shap...]
where the time goes in v3:
time: 20.4 us; the launch traced here: 20.2 us
  Pallas kernels  19.5 us (96%)
  local copies, waits for them, and re-layouts  0.71 us (3%)
    pallas_call x1, Pallas kernels, shards(): pl.pallas_call(functools.partial(kernel, n_row, n_col, n_layer), out_shap...  19.5 us
    unnamed x1, local copies, waits for them, and re-layouts  0.71 us

profile of v3, /device:TPU:0, one launch (start us, length us, event | category | flops | bytes accessed | tf_op | source)
XLA Modules:
  0.0 20.2 jit_solution(9259747182230734102)
XLA Ops:
  0.0 19.5 %shard_map.46 = bf16[256,512]{1,0:T(8,128)(2,1)S(1)} custom-call(bf16[1024,512]{1,0:T(8,128)(2,1)} %x_ref.1, bf16[1024,512]{1,0:T(8,128)(2,1)} %s_ref.1, s32[16,16]{1,0:T(8,128)} %pattern_hbm.1, s32[16,16]{1,0:T(8,128)} %keep_hbm.1), custom_call_target="tpu_custom_call" | custom-call | flops 536870912 | bytes 1572864 | tf_op jit(solution)/shard_map/pallas_call | solution.py:239
  19.5 0.7 %copy.6 = bf16[256,512]{1,0:T(8,128)(2,1)} copy(bf16[256,512]{1,0:T(8,128)(2,1)S(1)} %shard_map.46) | data formatting | bytes 524288

commit v4 on v3

--- a/solution.py
+++ b/solution.py
@@ -52,7 +52,8 @@
     mate_col = col + 1 - 2 * core
     n_chip = n_col // 2
     relayed = n_chunk // 2 - 3
-    direct = n_chunk - relayed
+    direct = relayed + 1
+    tail = pl.ds(relayed * ch, (n_chunk - 2 * relayed) * ch)
 
     def peer_row(d):
         return lax.rem(row + d, n_row)
@@ -91,7 +92,7 @@
     y = {}
     for j in range(direct):
         for d in range(1, n_row):
-            rows = chunk_at(j, half)
+            rows = chunk_at(j, half) if j < relayed else tail
             y[d, j] = pltpu.make_async_remote_copy(
                 src_ref=sbuf.at[row, rows, :],
                 dst_ref=sbuf.at[row, rows, :],
@@ -190,7 +191,7 @@
         if j == relayed - 3:
             pass_x()
             x_passed = True
-        if j == relayed:
+        if j == relayed - 1:
             mask_x()
             acc[...] = sum((term(row, g) for g in range(1, n_group)), term(row, 0))
             masked = True
@@ -199,6 +200,9 @@
                 for d in range(1, n_row):
                     acc[...] += term(from_row(d), group_of(done, half))
                 done += 1
+    for i in range(done, n_group // 2):
+        for d in range(1, n_row):
+            acc[...] += term(from_row(d), group_of(i, half))
     for i in range(n_group // 2 - 1):
         for d in range(1, n_row):
             for j in range(i * PIECES, (i + 1) * PIECES):
@@ -233,7 +237,7 @@
     m = rows // n_layer
     n_chunk = sr // GROUP * PIECES
     relayed = n_chunk // 2 - 3
-    direct = n_chunk - relayed
+    direct = relayed + 1
     dma = pltpu.SemaphoreType.DMA
     order = n_col * kc
     return pl.pallas_call(

time: 20.4 us -> 20.3 us (level)
  no operation moved by 1% of the time
where the time goes in v4:
time: 20.3 us; the launch traced here: 20.1 us
  Pallas kernels  19.4 us (96%)
  local copies, waits for them, and re-layouts  0.71 us (3%)
    pallas_call x1, Pallas kernels, shards(): pl.pallas_call(functools.partial(kernel, n_row, n_col, n_layer), out_shap...  19.4 us
    unnamed x1, local copies, waits for them, and re-layouts  0.71 us

profile of v4, /device:TPU:0, one launch (start us, length us, event | category | flops | bytes accessed | tf_op | source)
XLA Modules:
  0.0 20.1 jit_solution(11555287217983861711)
XLA Ops:
  0.0 19.4 %shard_map.46 = bf16[256,512]{1,0:T(8,128)(2,1)S(1)} custom-call(bf16[1024,512]{1,0:T(8,128)(2,1)} %x_ref.1, bf16[1024,512]{1,0:T(8,128)(2,1)} %s_ref.1, s32[16,16]{1,0:T(8,128)} %pattern_hbm.1, s32[16,16]{1,0:T(8,128)} %keep_hbm.1), custom_call_target="tpu_custom_call" | custom-call | flops 536870912 | bytes 1572864 | tf_op jit(solution)/shard_map/pallas_call | solution.py:243
  19.4 0.7 %copy.6 = bf16[256,512]{1,0:T(8,128)(2,1)} copy(bf16[256,512]{1,0:T(8,128)(2,1)S(1)} %shard_map.46) | data formatting | bytes 524288
